TPU v7x, 512 devices: a whole 4x4x16 slice. The times are simulated.
512 devices in a mesh: dp: 16 (over z_hi, x, core), mp: 32 (over y, z_lo).
Axes of the slice: x: 4, y: 4, z: 16 (z_hi: 2, z_lo: 8; z = z_hi * 8 + z_lo), core: 2. Of those that a mesh axis runs over, the one named last changes fastest.
Arguments:
- accumulated: bfloat16 [16384, 28672], P('dp', 'mp'), may hold values from -6 to 6
- signs: int32 [8192], replicated, may hold values from 0 to 1
- q_start: bfloat16 [28672, 128], P('mp'), may hold values from -6 to 6
Outputs:
- new_error: bfloat16 [16384, 28672], P('dp', 'mp')
- p_basis: float32 [16384, 128], P('dp')
- q_factor: float32 [28672, 128], P('mp')
Inputs may be any that keep to these rules, and one draw needn't show every extreme that they name: `signs`: 1 keeps a row's sign, 0 negates it.
All inputs are finite; a program needn't handle non-finite values.
Results may differ from a plain program's by a relative error of at most 0.0053.
Values may be sent and summed in bfloat16 or wider, within the bound.
A program may use at most 64 MiB of HBM per device.

v0:
```python
import math

import jax
import jax.numpy as jnp
from jax import lax
from jax.sharding import PartitionSpec as P

REPLICAS = 2


def from_partner(block, axis, distance):
    count = lax.axis_size(axis)
    route = []
    for low in range(count):
        high = low | 1 << distance
        if high != low and high < count:
            route += [(low, high), (high, low)]
    return lax.ppermute(block, axis, route)


def sylvester(size):
    index = jnp.arange(size, dtype=jnp.int32)
    both = index[:, None] & index[None, :]
    parity = jnp.zeros((size, size), jnp.int32)
    for shift in range(max(size.bit_length() - 1, 1)):
        parity = parity ^ both >> shift & 1
    return (1 - 2 * parity).astype(jnp.float32)


def rotate(block):
    total_rows, width = block.shape
    factors = []
    remaining = total_rows
    while remaining > 1:
        factor = min(32, remaining)
        factors.append(factor)
        remaining = remaining // factor
    cube = block.reshape(tuple(factors) + (width,))
    for which_axis, factor in enumerate(factors):
        cube = jnp.tensordot(
            sylvester(factor), cube, axes=([1], [which_axis]), precision=lax.Precision.HIGHEST
        )
        cube = jnp.moveaxis(cube, 0, which_axis)
    return cube.reshape(total_rows, width)


def local(accumulated, signs, q_start):
    local_rows, columns = accumulated.shape
    dp_count = lax.axis_size("dp")
    group_size = dp_count // REPLICAS
    cross_bits = group_size.bit_length() - 1
    dp_index = lax.axis_index("dp")
    position = dp_index % group_size
    first_copy = jnp.where(dp_index < group_size, 1.0, 0.0).astype(jnp.float32)
    local_signs = lax.dynamic_slice_in_dim(signs, position * local_rows, local_rows)
    flipped = jnp.where(local_signs[:, None] == 1, accumulated, -accumulated)
    field = rotate(flipped.astype(jnp.float32))
    for bit_number in range(cross_bits):
        partner = from_partner(field, "dp", bit_number)
        upper_half = dp_index >> bit_number & 1 == 1
        field = jnp.where(upper_half, partner - field, field + partner)
    rotated = (field * (1.0 / math.sqrt(local_rows * group_size))).astype(jnp.bfloat16)
    rotated = lax.optimization_barrier(rotated)
    local_proj = jnp.dot(rotated, q_start, preferred_element_type=jnp.float32)
    projected = lax.psum(local_proj, "mp")
    bit_number = 3
    projected = projected + from_partner(projected, "dp", bit_number)
    own_gram = jnp.dot(projected.T, projected, precision=lax.Precision.HIGHEST) * first_copy
    gram = lax.psum(own_gram, "dp")
    lower = jnp.linalg.cholesky(gram)
    p_basis = jax.scipy.linalg.solve_triangular(lower, projected.T, lower=True).T
    basis16 = p_basis.astype(jnp.bfloat16)
    right_part = jnp.einsum("rc,rk->ck", rotated, basis16, preferred_element_type=jnp.float32)
    q_factor = lax.psum(right_part, "dp") / REPLICAS
    q16 = q_factor.astype(jnp.bfloat16)
    approx = jnp.einsum("rk,ck->rc", basis16, q16, preferred_element_type=jnp.float32)
    new_error = (rotated.astype(jnp.float32) - approx).astype(jnp.bfloat16)
    return (new_error, p_basis, q_factor)


def solution(mesh):
    in_specs = (P("dp", "mp"), P(), P("mp", None))
    out_specs = (P("dp", "mp"), P("dp", None), P("mp", None))
    return jax.shard_map(local, mesh=mesh, in_specs=in_specs, out_specs=out_specs, check_vma=False)
```

profile of v0, /device:TPU:1, one launch (start us, length us, event | category | flops | bytes accessed | tf_op | source)
XLA Modules:
  0.0 1229.9 jit_solution(9110412983903951247)
XLA Ops:
  7.2 0.0 copy-start
  7.2 0.0 all-reduce.4.cloned.1.call-start
  7.2 0.7 dynamic-slice_compare_fusion
  8.0 1.8 negate_select_fusion
  9.8 1.8 fusion.2
  11.6 7.0 fusion
  18.6 8.8 collective-permute-start
  27.4 6.4 collective-permute-done
  33.7 5.3 add_select_fusion.1
  39.1 1.9 collective-permute-start.1
  41.0 80.8 %collective-permute-done.1 = f32[1024,896]{1,0:T(8,128)} collective-permute-done((f32[1024,896]{1,0:T(8,128)}, f32[1024,896]{1,0:T(8,128)}, u32[]{:S(2)}, u32[]{:S(2)}) %collective-permute-start.1) | collective-permute-done | bytes 3670048 | tf_op jit(solution)/shard_map/ppermute | solution.py:18
  121.8 5.3 add_select_fusion
  127.1 1.9 collective-permute-start.2
  129.1 81.4 %collective-permute-done.2 = f32[1024,896]{1,0:T(8,128)} collective-permute-done((f32[1024,896]{1,0:T(8,128)}, f32[1024,896]{1,0:T(8,128)}, u32[]{:S(2)}, u32[]{:S(2)}) %collective-permute-start.2) | collective-permute-done | bytes 3670048 | tf_op jit(solution)/shard_map/ppermute | solution.py:18
  210.5 3.7 multiply_convert_fusion
  214.2 0.0 copy-done
  214.2 1.4 fusion.26
  215.6 0.0 all-reduce.4.cloned.1.call-update
  215.7 0.0 all-reduce.6.cloned.1.call-start
  215.7 432.9 %all-reduce.4.cloned.1.call-done = f32[1024,128]{1,0:T(8,128)} async-done(((f32[1024,128]{1,0:T(8,128)}), f32[1024,128]{1,0:T(8,128)}) %all-reduce.4.cloned.1.call-update) | async-done | bytes 524304 | tf_op jit(solution)/shard_map/psum | solution.py:65
  648.6 13.0 %collective-permute-start.3 = (f32[1024,128]{1,0:T(8,128)}, f32[1024,128]{1,0:T(8,128)S(1)}, u32[]{:S(2)}, u32[]{:S(2)}) collective-permute-start(f32[1024,128]{1,0:T(8,128)} %all-reduce.4.cloned.1.call-done), channel_id=1, source_target_pairs={{0,256},{256,0},{32,288},{288,32},{64,320},{320,64},{96,352},{352,... | collective-permute-start | bytes 1572872 | tf_op jit(solution)/shard_map/ppermute | solution.py:18
  661.6 12.9 %collective-permute-done.3 = f32[1024,128]{1,0:T(8,128)S(1)} collective-permute-done((f32[1024,128]{1,0:T(8,128)}, f32[1024,128]{1,0:T(8,128)S(1)}, u32[]{:S(2)}, u32[]{:S(2)}) %collective-permute-start.3) | collective-permute-done | bytes 524320 | tf_op jit(solution)/shard_map/ppermute | solution.py:18
  674.5 1.1 add.42
  675.6 1.6 convolution_multiply_fusion
  677.2 0.0 all-reduce.6.cloned.1.call-update
  677.2 0.2 all-reduce.8.cloned.1.call-start
  677.5 263.6 %all-reduce.6.cloned.1.call-done = f32[128,128]{0,1:T(8,128)} async-done(((f32[128,128]{0,1:T(8,128)}), f32[128,128]{0,1:T(8,128)}) %all-reduce.6.cloned.1.call-update) | async-done | bytes 65552 | tf_op jit(solution)/shard_map/psum | solution.py:69
  941.1 0.9 copy.7
  942.0 0.9 fusion.11
  942.9 11.7 cholesky.16
  954.6 0.6 compare_reduce_fusion
  955.3 0.7 fusion.8
  955.9 9.8 custom-call.7
  965.7 0.6 fusion.9
  966.3 0.0 copy-start.1
  966.3 1.4 fusion.6
  967.8 0.0 all-reduce.8.cloned.1.call-update
  967.8 252.6 %all-reduce.8.cloned.1.call-done = f32[896,128]{1,0:T(8,128)} async-done(((f32[896,128]{1,0:T(8,128)}), f32[896,128]{1,0:T(8,128)}) %all-reduce.8.cloned.1.call-update) | async-done | bytes 458768 | tf_op jit(solution)/shard_map/psum | solution.py:74
  1220.4 1.0 broadcast_multiply_fusion
  1221.5 0.0 copy-start.2
  1221.5 1.9 subtract_convert_fusion
  1223.3 0.0 copy-done.1
  1223.3 0.0 copy-done.2
  (1 shorter events, 0.0 us)
Async XLA Ops:
  7.2 207.0 %copy-start = (bf16[896,128]{1,0:T(8,128)(2,1)S(1)}, bf16[896,128]{1,0:T(8,128)(2,1)}, u32[]{:S(2)}) copy-start(bf16[896,128]{1,0:T(8,128)(2,1)} %param.5) | copy-start | bytes 688132
  7.2 641.4 %all-reduce.4.cloned.1.call-start = ((), (), s32[]{:S(2)}) async-start(), calls=%async_computation | async-start | bytes 1048576 | tf_op jit(solution)/shard_map/psum | solution.py:65
  18.6 15.1 %collective-permute-start = (f32[1024,896]{1,0:T(8,128)}, f32[1024,896]{1,0:T(8,128)}, u32[]{:S(2)}, u32[]{:S(2)}) collective-permute-start(f32[1024,896]{1,0:T(8,128)} %bitcast.3), channel_id=1, source_target_pairs={{0,32},{32,0},{64,96},{96,64},{128,160},{160,128},{192,224},{224,1... | collective-permute-start | bytes 11010056 | tf_op jit(solution)/shard_map/ppermute | solution.py:18
  39.1 82.7 %collective-permute-start.1 = (f32[1024,896]{1,0:T(8,128)}, f32[1024,896]{1,0:T(8,128)}, u32[]{:S(2)}, u32[]{:S(2)}) collective-permute-start(f32[1024,896]{1,0:T(8,128)} %add_select_fusion.1), channel_id=1, source_target_pairs={{0,64},{64,0},{32,96},{96,32},{128,192},{192,128},{160,224},{224,1... | collective-permute-start | bytes 11010056 | tf_op jit(solution)/shard_map/ppermute | solution.py:18
  127.1 83.3 %collective-permute-start.2 = (f32[1024,896]{1,0:T(8,128)}, f32[1024,896]{1,0:T(8,128)}, u32[]{:S(2)}, u32[]{:S(2)}) collective-permute-start(f32[1024,896]{1,0:T(8,128)} %add_select_fusion), channel_id=1, source_target_pairs={{0,128},{128,0},{32,160},{160,32},{64,192},{192,64},{96,224},{224,... | collective-permute-start | bytes 11010056 | tf_op jit(solution)/shard_map/ppermute | solution.py:18
  215.7 725.4 %all-reduce.6.cloned.1.call-start = ((), (), s32[]{:S(2)}) async-start(), calls=%async_computation.1 | async-start | bytes 131072 | tf_op jit(solution)/shard_map/psum | solution.py:69
  648.6 25.9 %collective-permute-start.3 = (f32[1024,128]{1,0:T(8,128)}, f32[1024,128]{1,0:T(8,128)S(1)}, u32[]{:S(2)}, u32[]{:S(2)}) collective-permute-start(f32[1024,128]{1,0:T(8,128)} %all-reduce.4.cloned.1.call-done), channel_id=1, source_target_pairs={{0,256},{256,0},{32,288},{288,32},{64,320},{320,64},{96,352},{352,... | collective-permute-start | bytes 1572872 | tf_op jit(solution)/shard_map/ppermute | solution.py:18
  677.2 543.2 %all-reduce.8.cloned.1.call-start = ((), (), s32[]{:S(2)}) async-start(), calls=%async_computation.2 | async-start | bytes 917504 | tf_op jit(solution)/shard_map/psum | solution.py:74
  966.3 257.0 %copy-start.1 = (f32[1024,128]{1,0:T(8,128)}, f32[1024,128]{1,0:T(8,128)S(1)}, u32[]{:S(2)}) copy-start(f32[1024,128]{1,0:T(8,128)S(1)} %fusion.9) | copy-start | bytes 1572868
  1221.5 1.9 copy-start.2
Sparse Core Ops, SparseCore 0:
  215.8 432.7 all-reduce.3
  677.4 263.6 all-reduce.5
  967.9 252.4 all-reduce.7
where the time goes:
time: 1230 us
  waiting for transfers between devices  1130 us (92%)
  other arithmetic  42.8 us (3%)
  starting transfers between devices  25.9 us (2%)
  matrix products  15.7 us (1%)
  between operations  13.9 us (1%)
    psum x1, waiting for transfers between devices, local(): projected = lax.psum(local_proj, 'mp')  433 us
    psum x1, waiting for transfers between devices, local(): gram = lax.psum(own_gram, 'dp')  264 us
    psum x1, waiting for transfers between devices, local(): q_factor = lax.psum(right_part, 'dp') / REPLICAS  253 us
    ppermute x4, waiting for transfers between devices, from_partner(): return lax.ppermute(block, axis, route)  181 us
    ppermute x4, starting transfers between devices, from_partner(): return lax.ppermute(block, axis, route)  25.6 us
  transfers between devices with their start and end apart: 7, of which 7 were waited for; matrix products, arithmetic and copies ran while one was open for 0% of the time, Pallas kernels for 0%

commit v1 on v0

v1 whole, which is shorter than its diff:
```python
import functools
import math

import jax
import jax.numpy as jnp
from jax import lax
from jax.experimental import pallas as pl
from jax.experimental.pallas import tpu as pltpu
from jax.sharding import PartitionSpec as P

MESH = pl.DeviceIdType.MESH
HIGH = lax.Precision.HIGHEST
REPLICAS, NX, NCORE, NY, ZLO = 2, 4, 2, 4, 8
NZ = REPLICAS * ZLO
NPOS = NX * NCORE
LANES = 128
SMALL = 256
F32, BF16 = jnp.float32, jnp.bfloat16


def parity_sign(rows, cols):
    i = lax.broadcasted_iota(jnp.int32, (rows, cols), 0)
    j = lax.broadcasted_iota(jnp.int32, (rows, cols), 1)
    both = i & j
    for shift in (4, 2, 1):
        both = both ^ (both >> shift)
    return (1 - 2 * (both & 1)).astype(F32)


def four(t):
    a, b, c, d = t[0] + t[1], t[0] - t[1], t[2] + t[3], t[2] - t[3]
    return (a + c, b + d, a - c, b - d)


def dot(a, b, **kw):
    return jnp.dot(a, b, preferred_element_type=F32, **kw)


def dot_t(a, b):
    return lax.dot_general(a, b, (((0,), (0,)), ((), ())), preferred_element_type=F32)


def kernel(a_ref, signs_ref, q_ref, err_ref, basis_ref, qf_ref,
           par, us, r1, wo, rot, hs, yp, ys, ybuf, zs, zbuf, vbuf, vz, yg, vg,
           gs, gcore, gsum, gx, ztp, ztc, zh, ztx, zx, ztz, zta, m_ref, n_ref,
           send, recv, rawsem, asem, bsem):
    dp, mp = lax.axis_index("dp"), lax.axis_index("mp")
    zhi, pos = dp // NPOS, dp % NPOS
    x, core = pos // NCORE, pos % NCORE
    y, zlo = mp // ZLO, mp % ZLO
    z = zhi * ZLO + zlo
    rows, cols = a_ref.shape
    groups = cols // LANES
    quarter = rows // NX
    yrows = rows // NY
    zrows = yrows // NZ
    rank = q_ref.shape[1]
    scale = 1.0 / math.sqrt(rows * NPOS)

    def at_y(k):
        yy = (y + k) % NY
        return yy, (dp, yy * ZLO + zlo)

    def at_z(k):
        zz = (z + k) % NZ
        return zz, ((zz // ZLO) * NPOS + pos, y * ZLO + zz % ZLO)

    def at_pos(k):
        pp = (pos + k) % NPOS
        return (zhi * NPOS + pp, mp)

    def at_x(k):
        xx = (x + k) % NX
        return xx, (zhi * NPOS + xx * NCORE + core, mp)

    other_core = (zhi * NPOS + x * NCORE + 1 - core, mp)
    other_rep = ((1 - zhi) * NPOS + pos, mp)

    def start(src, dst, s, r, device):
        pltpu.make_async_remote_copy(
            src_ref=src, dst_ref=dst, send_sem=s, recv_sem=r, device_id=device, device_id_type=MESH
        ).start()

    def wait(ref, sem):
        pltpu.make_async_copy(ref, ref, sem).wait()

    sent = []

    def lanes(g):
        return pl.ds(g * LANES, LANES)

    barrier = pltpu.get_barrier_semaphore()
    partners = [at_y(k)[1] for k in range(1, NY)] + [at_z(k)[1] for k in range(1, NZ)]
    partners += [at_pos(k) for k in range(1, NPOS)]
    for device in partners:
        pl.semaphore_signal(barrier, inc=1, device_id=device, device_id_type=MESH)

    yp[...] = dot(a_ref[...], q_ref[...])
    ys[...] = yp[...].astype(BF16)
    small = parity_sign(SMALL, SMALL)
    mine = (2 * signs_ref[pl.ds(pl.multiple_of(pos * 8, 8), 8), :] - 1).astype(F32)
    theirs_at = pos + 1 - 2 * core
    theirs = (2 * signs_ref[pl.ds(pl.multiple_of(theirs_at * 8, 8), 8), :] - 1).astype(F32)
    core_sign = (1 - 2 * core).astype(F32)
    for a in range(NX):
        row = jnp.concatenate([mine[2 * a : 2 * a + 1], mine[2 * a + 1 : 2 * a + 2]], axis=1)
        hs[a] = (small * (row * core_sign)).astype(BF16)
        row = jnp.concatenate([theirs[2 * a : 2 * a + 1], theirs[2 * a + 1 : 2 * a + 2]], axis=1)
        hs[NX + a] = (small * row).astype(BF16)

    pl.semaphore_wait(barrier, len(partners))

    for g in range(groups):
        start(a_ref.at[:, lanes(g)], par.at[:, lanes(g)], send.at[0], rawsem.at[g], other_core)
    sent.append((a_ref, 0))

    for k in range(1, NY):
        yy, device = at_y(k)
        start(ys.at[pl.ds(pl.multiple_of(yy * yrows, yrows), yrows), :], ybuf.at[k - 1],
              send.at[1], recv.at[1], device)
    sent.append((ybuf, 1))

    def transform(g):
        wait(par.at[:, lanes(g)], rawsem.at[g])
        t = []
        for a in range(NX):
            part = pl.ds(a * SMALL, SMALL)
            t.append(dot(hs[a], a_ref[part, lanes(g)]) + dot(hs[NX + a], par[part, lanes(g)]))
        for s, u in enumerate(four(t)):
            us[s, :, lanes(g)] = u.astype(BF16)
        r1[x, :, lanes(g)] = us[x, :, lanes(g)]
        for k in range(1, NX):
            xx, device = at_x(k)
            start(us.at[xx, :, lanes(g)], r1.at[x, :, lanes(g)], send.at[2], asem.at[g], device)

    def mix(g):
        wait(r1.at[0 : NX - 1, :, lanes(g)], asem.at[g])
        u = [r1[s, :, lanes(g)].astype(F32) for s in range(NX)]
        for s, w in enumerate(four(u)):
            wo[s, :, lanes(g)] = (w * scale).astype(BF16)
        rot[x, :, lanes(g)] = wo[x, :, lanes(g)]
        for k in range(1, NX):
            xx, device = at_x(k)
            start(wo.at[xx, :, lanes(g)], rot.at[x, :, lanes(g)], send.at[3], bsem.at[g], device)

    for g in range(3):
        transform(g)

    wait(ybuf, recv.at[1])
    total = yp[pl.ds(pl.multiple_of(y * yrows, yrows), yrows), :]
    for k in range(NY - 1):
        total = total + ybuf[k].astype(F32)
    zs[...] = total.astype(BF16)
    yp[0:yrows, :] = total
    for k in range(1, NZ):
        zz, device = at_z(k)
        start(zs.at[pl.ds(pl.multiple_of(zz * zrows, zrows), zrows), :], zbuf.at[k - 1],
              send.at[4], recv.at[4], device)
    sent.append((zbuf, 4))

    for g in range(3, groups):
        transform(g)
    for s in (2, 3):
        sent.append((r1.at[0 : NX - 1], s))

    wait(zbuf, recv.at[4])
    total = yp[pl.ds(pl.multiple_of(z * zrows, zrows), zrows), :]
    for k in range(NZ - 1):
        total = total + zbuf[k].astype(F32)
    own_rows = pl.multiple_of(y * yrows + z * zrows, zrows)
    yg[pl.ds(own_rows, zrows), :] = total.astype(BF16)
    for k in range(1, NZ):
        _, device = at_z(k)
        own = yg.at[pl.ds(own_rows, zrows), :]
        start(own, own, send.at[5], recv.at[5], device)
    sent.append((zbuf, 5))

    line = (2 * signs_ref[pl.ds(pos * 8 + own_rows // LANES, 1), :] - 1).astype(F32)
    spot = lax.broadcasted_iota(jnp.int32, (zrows, LANES), 0) + own_rows % LANES
    lane = lax.broadcasted_iota(jnp.int32, (zrows, LANES), 1)
    sign = jnp.sum(jnp.where(lane == spot, line, 0.0), axis=1, keepdims=True)
    vbuf[pos] = total * sign
    for k in range(1, NPOS):
        start(vbuf.at[pos], vbuf.at[pos], send.at[6], recv.at[6], at_pos(k))
    sent.append((vbuf.at[0 : NPOS - 1], 6))

    wait(zbuf, recv.at[5])
    for k in range(1, NY):
        _, device = at_y(k)
        own = yg.at[pl.ds(pl.multiple_of(y * yrows, yrows), yrows), :]
        start(own, own, send.at[7], recv.at[7], device)
    sent.append((ybuf, 7))

    wait(vbuf.at[0 : NPOS - 1], recv.at[6])
    mixed = jnp.zeros((zrows, rank), F32)
    for s in range(NPOS):
        bits = (pos % 2) * (s % 2) + (pos // 2 % 2) * (s // 2 % 2) + (pos // 4) * (s // 4)
        mixed = mixed + vbuf[s] * (1 - 2 * (bits % 2)).astype(F32)
    vg[pl.ds(own_rows, zrows), :] = mixed.astype(BF16)
    for k in range(1, NZ):
        _, device = at_z(k)
        own = vg.at[pl.ds(own_rows, zrows), :]
        start(own, own, send.at[8], recv.at[8], device)
    sent.append((zbuf, 8))

    wait(ybuf, recv.at[7])
    gs[...] = dot_t(yg[...], yg[...])
    start(gs, gcore, send.at[9], recv.at[9], other_core)
    sent.append((gs, 9))
    ztp[...] = dot_t(yg[...], a_ref[...])
    half = rank // NCORE
    theirs_half = pl.ds(pl.multiple_of((1 - core) * half, half), half)
    start(ztp.at[theirs_half, :], ztc, send.at[10], recv.at[10], other_core)
    sent.append((ztc, 10))

    wait(zbuf, recv.at[8])
    for k in range(1, NY):
        _, device = at_y(k)
        own = vg.at[pl.ds(pl.multiple_of(y * yrows, yrows), yrows), :]
        start(own, own, send.at[11], recv.at[11], device)
    sent.append((ybuf, 11))

    wait(gcore, recv.at[9])
    gx[x] = gs[...] + gcore[...]
    for k in range(1, NX):
        _, device = at_x(k)
        start(gx.at[x], gx.at[x], send.at[12], recv.at[12], device)
    sent.append((gx.at[0 : NX - 1], 12))

    wait(ztc, recv.at[10])
    part = rank // NPOS
    zh[...] = ztp[pl.ds(pl.multiple_of(core * half, half), half), :] + ztc[...]
    for k in range(1, NX):
        xx, device = at_x(k)
        start(zh.at[pl.ds(pl.multiple_of(xx * part, part), part), :], ztx.at[k - 1],
              send.at[13], recv.at[13], device)
    sent.append((ztx, 13))

    for g in range(groups):
        mix(g)

    wait(ztx, recv.at[13])
    total = zh[pl.ds(pl.multiple_of(x * part, part), part), :]
    for k in range(NX - 1):
        total = total + ztx[k]
    zx[...] = total
    start(zx, ztz, send.at[14], recv.at[14], other_rep)
    sent.append((zx, 14))

    wait(gx.at[0 : NX - 1], recv.at[12])
    m_ref[...] = gx[0] + gx[1] + gx[2] + gx[3]
    ri = lax.broadcasted_iota(jnp.int32, (rank, rank), 0)
    ci = lax.broadcasted_iota(jnp.int32, (rank, rank), 1)
    n_ref[...] = jnp.where(ri == ci, 1.0, 0.0).astype(F32)

    def eliminate(j, carry):
        m = m_ref[...]
        row = m_ref[pl.ds(j, 1), :]
        nrow = n_ref[pl.ds(j, 1), :]
        pivot = jnp.sum(jnp.where(ci[0:1] == j, row, 0.0), axis=1, keepdims=True)
        col = jnp.sum(jnp.where(ci == j, m, 0.0), axis=1, keepdims=True)
        col = jnp.where(ri[:, 0:1] > j, col / pivot, 0.0)
        m_ref[...] = m - col * row
        n_ref[...] = n_ref[...] - col * nrow
        return carry

    lax.fori_loop(0, rank, eliminate, 0)
    pivots = jnp.sum(jnp.where(ri == ci, m_ref[...], 0.0), axis=1, keepdims=True)
    inverse = n_ref[...] * (1.0 / jnp.sqrt(pivots))

    wait(ztz, recv.at[14])
    rank_rows = pl.multiple_of(core * half + x * part, part)
    zta[pl.ds(rank_rows, part), :] = zx[...] + ztz[...]
    for k in range(1, NX):
        _, device = at_x(k)
        own = zta.at[pl.ds(rank_rows, part), :]
        start(own, own, send.at[15], recv.at[15], device)
    sent.append((ztx, 15))

    wait(ybuf, recv.at[11])
    t = []
    small16 = small.astype(BF16)
    for a in range(NX):
        t.append(dot(small16, vg[a * SMALL : (a + 1) * SMALL, :]))
    for a, v in enumerate(four(t)):
        basis_ref[a * SMALL : (a + 1) * SMALL, :] = lax.dot_general(
            v * scale, inverse, (((1,), (1,)), ((), ())), precision=HIGH, preferred_element_type=F32
        )

    wait(ztx, recv.at[15])
    own = zta.at[pl.ds(pl.multiple_of(core * half, half), half), :]
    start(own, own, send.at[16], recv.at[16], other_core)
    sent.append((ztc, 16))
    wait(ztc, recv.at[16])
    right = dot(inverse, zta[...], precision=HIGH) * (1.0 / REPLICAS)
    for g in range(groups):
        qf_ref[lanes(g), :] = right[:, g * LANES : (g + 1) * LANES].T
    right16 = right.astype(BF16)

    for g in range(groups):
        wait(rot.at[0 : NX - 1, :, lanes(g)], bsem.at[g])
    for a in range(NX):
        part_rows = pl.ds(a * SMALL, SMALL)
        approx = dot(basis_ref[part_rows, :].astype(BF16), right16)
        err_ref[part_rows, :] = (rot[a].astype(F32) - approx).astype(BF16)
    for ref, s in sent:
        wait(ref, send.at[s])


def local(accumulated, signs, q_start):
    rows, cols = accumulated.shape
    rank = q_start.shape[1]
    quarter, yrows = rows // NX, rows // NY
    zrows, half, part = yrows // NZ, rank // NCORE, rank // NPOS
    groups = cols // LANES
    vmem = pl.BlockSpec(memory_space=pltpu.VMEM)
    dma = pltpu.SemaphoreType.DMA
    scratch = [
        ((rows, cols), BF16), ((NX, quarter, cols), BF16), ((NX, quarter, cols), BF16),
        ((NX, quarter, cols), BF16), ((NX, quarter, cols), BF16), ((2 * NX, SMALL, SMALL), BF16),
        ((rows, rank), F32), ((rows, rank), BF16), ((NY - 1, yrows, rank), BF16),
        ((yrows, rank), BF16), ((NZ - 1, zrows, rank), BF16), ((NPOS, zrows, rank), F32),
        ((zrows, rank), BF16), ((rows, rank), BF16), ((rows, rank), BF16),
        ((rank, rank), F32), ((rank, rank), F32), ((rank, rank), F32), ((NX, rank, rank), F32),
        ((rank, cols), F32), ((half, cols), F32), ((half, cols), F32), ((NX - 1, part, cols), F32),
        ((part, cols), F32), ((part, cols), F32), ((rank, cols), F32),
        ((rank, rank), F32), ((rank, rank), F32),
    ]
    return pl.pallas_call(
        kernel,
        out_shape=(
            jax.ShapeDtypeStruct((rows, cols), BF16),
            jax.ShapeDtypeStruct((rows, rank), F32),
            jax.ShapeDtypeStruct((cols, rank), F32),
        ),
        in_specs=[vmem] * 3,
        out_specs=(vmem,) * 3,
        scratch_shapes=[pltpu.VMEM(shape, kind) for shape, kind in scratch]
        + [dma((17,)), dma((17,)), dma((groups,)), dma((groups,)), dma((groups,))],
        compiler_params=pltpu.CompilerParams(
            collective_id=0, has_side_effects=True, vmem_limit_bytes=48 * 1024 * 1024
        ),
        name="powersgd",
    )(accumulated, signs.reshape(-1, LANES), q_start)


def solution(mesh):
    in_specs = (P("dp", "mp"), P(), P("mp", None))
    out_specs = (P("dp", "mp"), P("dp", None), P("mp", None))
    return jax.shard_map(local, mesh=mesh, in_specs=in_specs, out_specs=out_specs, check_vma=False)
```

time: 1230 us -> 87.2 us (0.07)
  waiting for transfers between devices: 1130 us -> 0 us
  Pallas kernels: 0 us -> 80.3 us
  other arithmetic: 42.8 us -> 0 us
  starting transfers between devices: 25.9 us -> 0 us
  matrix products: 15.7 us -> 0 us
  between operations: 13.9 us -> 0.65 us
    psum x3 -> x0, waiting for transfers between devices: 949 us -> none  [the longest x1 433 us: local(): projected = lax.psum(local_proj, 'mp')]
    ppermute x4 -> x0, waiting for transfers between devices: 181 us -> none  [from_partner(): return lax.ppermute(block, axis, route)]
    pallas_call x0 -> x1, Pallas kernels: none -> 80.3 us  [local(): pl.pallas_call(kernel, out_shape=(jax.ShapeDtypeStruct((rows, cols), BF16...]
    ppermute x4 -> x0, starting transfers between devices: 25.6 us -> none  [from_partner(): return lax.ppermute(block, axis, route)]
    another operation x5 -> x0, other arithmetic: 22.9 us -> none  [the longest x3 12.4 us: local(): lower = jnp.linalg.cholesky(gram)]
    dot_general x6 -> x0, matrix products: 15.2 us -> none  [the longest x2 8.76 us: rotate(): jnp.tensordot(sylvester(factor), cube, axes=([1], [which_axis]), precisio...]
    select_n x3 -> x0, other arithmetic: 12.5 us -> none  [the longest x2 10.6 us: local(): field = jnp.where(upper_half, partner - field, field + partner)]
  transfers between devices with their start and end apart: 7 -> 0, of which waited for: 7 -> 0; matrix products, arithmetic and copies ran while one was open for 0% -> 0% of each run, Pallas kernels for 0% -> 0%
where the time goes in v1:
time: 87.2 us; the launch traced here: 86.9 us
  Pallas kernels  80.3 us (92%)
  local copies, waits for them, and re-layouts  5.98 us (7%)
    pallas_call x1, Pallas kernels, local(): pl.pallas_call(kernel, out_shape=(jax.ShapeDtypeStruct((rows, cols), BF16...  80.3 us
    unnamed x9, local copies, waits for them, and re-layouts  5.98 us

profile of v1, /device:TPU:1, one launch (start us, length us, event | category | flops | bytes accessed | tf_op | source)
XLA Modules:
  0.0 86.9 jit_solution(4602959464634292025)
XLA Ops:
  0.6 0.0 copy-start
  0.6 1.5 %copy-done = bf16[1024,896]{1,0:T(8,128)(2,1)S(1)} copy-done((bf16[1024,896]{1,0:T(8,128)(2,1)S(1)}, bf16[1024,896]{1,0:T(8,128)(2,1)}, u32[]{:S(2)}) %copy-start) | copy-done | bytes 1835032
  2.1 0.0 copy-start.1
  2.1 0.9 %copy-done.1 = bf16[896,128]{1,0:T(8,128)(2,1)S(1)} copy-done((bf16[896,128]{1,0:T(8,128)(2,1)S(1)}, bf16[896,128]{1,0:T(8,128)(2,1)}, u32[]{:S(2)}) %copy-start.1) | copy-done | bytes 229400
  3.1 0.0 copy-start.2
  3.1 0.8 copy-done.2
  3.8 80.3 %powersgd.1 = (bf16[1024,896]{1,0:T(8,128)(2,1)S(1)}, f32[1024,128]{1,0:T(8,128)S(1)}, f32[896,128]{1,0:T(8,128)S(1)}) custom-call(bf16[1024,896]{1,0:T(8,128)(2,1)S(1)} %copy-done, s32[64,128]{1,0:T(8,128)S(1)} %bitcast.1, bf16[896,128]{1,0:T(8,128)(2,1)S(1)} %copy-done.1), custom_call_target="tpu_custom_call" | custom-call | tf_op jit(solution)/shard_map/powersgd/pallas_call | solution.py:329
  84.1 1.2 %copy.9 = bf16[1024,896]{1,0:T(8,128)(2,1)} copy(bf16[1024,896]{1,0:T(8,128)(2,1)S(1)} %get-tuple-element.6) | data formatting | bytes 3670016
  85.4 0.8 copy.10
  86.2 0.8 copy.11
Async XLA Ops:
  0.6 1.5 %copy-start = (bf16[1024,896]{1,0:T(8,128)(2,1)S(1)}, bf16[1024,896]{1,0:T(8,128)(2,1)}, u32[]{:S(2)}) copy-start(bf16[1024,896]{1,0:T(8,128)(2,1)} %a_ref.1) | copy-start | bytes 5505028
  2.1 0.9 %copy-start.1 = (bf16[896,128]{1,0:T(8,128)(2,1)S(1)}, bf16[896,128]{1,0:T(8,128)(2,1)}, u32[]{:S(2)}) copy-start(bf16[896,128]{1,0:T(8,128)(2,1)} %q_ref.1) | copy-start | bytes 688132
  3.1 0.8 copy-start.2

commit v2 on v1

v2 whole, which is shorter than its diff:
```python
import functools
import math

import jax
import jax.numpy as jnp
from jax import lax
from jax.experimental import pallas as pl
from jax.experimental.pallas import tpu as pltpu
from jax.sharding import PartitionSpec as P

MESH = pl.DeviceIdType.MESH
HIGH = lax.Precision.HIGHEST
REPLICAS, NX, NCORE, NY, ZLO = 2, 4, 2, 4, 8
NZ = REPLICAS * ZLO
NPOS = NX * NCORE
LANES = 128
FAR_FIRST = (8, 7, 9, 6, 10, 5, 11, 4, 12, 3, 13, 2, 14, 1, 15)
SMALL = 256
F32, BF16 = jnp.float32, jnp.bfloat16


def parity_sign(rows, cols):
    i = lax.broadcasted_iota(jnp.int32, (rows, cols), 0)
    j = lax.broadcasted_iota(jnp.int32, (rows, cols), 1)
    both = i & j
    for shift in (4, 2, 1):
        both = both ^ (both >> shift)
    return (1 - 2 * (both & 1)).astype(F32)


def four(t):
    a, b, c, d = t[0] + t[1], t[0] - t[1], t[2] + t[3], t[2] - t[3]
    return (a + c, b + d, a - c, b - d)


def dot(a, b, **kw):
    return jnp.dot(a, b, preferred_element_type=F32, **kw)


def dot_t(a, b):
    return lax.dot_general(a, b, (((0,), (0,)), ((), ())), preferred_element_type=F32)


def wide(v, width):
    return jnp.broadcast_to(v, (1, width))


def inverse_cholesky(m, out_ref, step):
    rank = m.shape[0]
    ri = lax.broadcasted_iota(jnp.int32, (rank, rank), 0)
    ci = lax.broadcasted_iota(jnp.int32, (rank, rank), 1)
    n = jnp.where(ri == ci, 1.0, 0.0).astype(F32)
    for j in range(0, rank, step):
        span = range(step)
        r = [m[j + a : j + a + 1, :] for a in span]
        s = [n[j + a : j + a + 1, :] for a in span]
        p = [[wide(r[a][:, j + b : j + b + 1], rank) if b >= a else None for b in span] for a in span]
        low = [[None] * step for _ in span]
        inv = [None] * step
        for a in span:
            inv[a] = 1.0 / p[a][a]
            for b in range(a + 1, step):
                low[b][a] = p[a][b] * inv[a]
                for c in range(b, step):
                    p[b][c] = p[b][c] - low[b][a] * p[a][c]
                r[b] = r[b] - low[b][a] * r[a]
                s[b] = s[b] - low[b][a] * s[a]
        w, v = [None] * step, [None] * step
        for a in reversed(span):
            w[a], v[a] = r[a] * inv[a], s[a] * inv[a]
            for b in range(a + 1, step):
                w[a] = w[a] - low[b][a] * w[b]
                v[a] = v[a] - low[b][a] * v[b]
        for a in span:
            out_ref[j + a : j + a + 1, :] = s[a] * (1.0 / jnp.sqrt(p[a][a]))
        if j + step < rank:
            cols = [jnp.broadcast_to(m[:, j + a : j + a + 1], m.shape) for a in span]
            for a in span:
                m = m - cols[a] * w[a]
                n = n - cols[a] * v[a]


def kernel(a_hbm, signs_hbm, q_hbm, err_ref, basis_ref, qf_ref,
           a_ref, signs_ref, q_ref,
           par, us, r1, wo, rot, hs, yp, ys, ybuf, zs, zbuf, vbuf, yg, vg,
           gs, gcore, gx, gall, ztp, ztc, zh, ztx, zx, ztz, zta, inv_ref,
           send, recv, rawsem, asem, bsem, insem):
    dp, mp = lax.axis_index("dp"), lax.axis_index("mp")
    zhi, pos = dp // NPOS, dp % NPOS
    x, core = pos // NCORE, pos % NCORE
    y, zlo = mp // ZLO, mp % ZLO
    z = zhi * ZLO + zlo
    rows, cols = a_ref.shape
    groups = cols // LANES
    yrows = rows // NY
    zrows = yrows // NZ
    rank = q_ref.shape[1]
    scale = 1.0 / math.sqrt(rows * NPOS)

    def at_y(k):
        yy = (y + k) % NY
        return yy, (dp, yy * ZLO + zlo)

    def at_z(k):
        zz = (z + k) % NZ
        return zz, ((zz // ZLO) * NPOS + pos, y * ZLO + zz % ZLO)

    def at_pos(k):
        return (zhi * NPOS + (pos + k) % NPOS, mp)

    def at_x(k):
        xx = (x + k) % NX
        return xx, (zhi * NPOS + xx * NCORE + core, mp)

    other_core = (zhi * NPOS + x * NCORE + 1 - core, mp)
    other_rep = ((1 - zhi) * NPOS + pos, mp)

    def start(src, dst, s, r, device):
        pltpu.make_async_remote_copy(
            src_ref=src, dst_ref=dst, send_sem=s, recv_sem=r, device_id=device, device_id_type=MESH
        ).start()

    def wait(ref, sem):
        pltpu.make_async_copy(ref, ref, sem).wait()

    def lanes(g):
        return pl.ds(g * LANES, LANES)

    def some(first, count):
        return pl.ds(pl.multiple_of(first, count), count)

    sent = []

    barrier = pltpu.get_barrier_semaphore()
    partners = [at_z(k)[1] for k in FAR_FIRST] + [at_y(k)[1] for k in range(1, NY)]
    partners += [at_pos(k) for k in range(1, NPOS)]
    for device in partners:
        pl.semaphore_signal(barrier, inc=1, device_id=device, device_id_type=MESH)

    loads = [pltpu.make_async_copy(src, dst, insem.at[i])
             for i, (src, dst) in enumerate(((signs_hbm, signs_ref), (q_hbm, q_ref), (a_hbm, a_ref)))]
    for load in loads:
        load.start()
    loads[0].wait()
    small = parity_sign(SMALL, SMALL)
    mine = (2 * signs_ref[some(pos * 8, 8), :] - 1).astype(F32)
    theirs = (2 * signs_ref[some((pos + 1 - 2 * core) * 8, 8), :] - 1).astype(F32)
    core_sign = (1 - 2 * core).astype(F32)
    for a in range(NX):
        row = jnp.concatenate([mine[2 * a : 2 * a + 1], mine[2 * a + 1 : 2 * a + 2]], axis=1)
        hs[a] = (small * (row * core_sign)).astype(BF16)
        row = jnp.concatenate([theirs[2 * a : 2 * a + 1], theirs[2 * a + 1 : 2 * a + 2]], axis=1)
        hs[NX + a] = (small * row).astype(BF16)
    loads[1].wait()
    loads[2].wait()
    yp[...] = dot(a_ref[...], q_ref[...])
    ys[...] = yp[...].astype(BF16)

    pl.semaphore_wait(barrier, len(partners))

    for k in (2, 1, 3):
        yy, device = at_y(k)
        start(ys.at[some(yy * yrows, yrows), :], ybuf.at[k - 1], send.at[1], recv.at[1], device)
    sent.append((ybuf, 1))

    for g in range(groups):
        start(a_ref.at[:, lanes(g)], par.at[g], send.at[0], rawsem.at[g], other_core)
    sent.append((par, 0))

    def transform(g):
        wait(par.at[g], rawsem.at[g])
        t = []
        for a in range(NX):
            part = pl.ds(a * SMALL, SMALL)
            t.append(dot(hs[a], a_ref[part, lanes(g)]) + dot(hs[NX + a], par[g, part, :]))
        for s, u in enumerate(four(t)):
            us[g, s] = u.astype(BF16)
        r1[g, x] = us[g, x]
        for k in range(1, NX):
            xx, device = at_x(k)
            start(us.at[g, xx], r1.at[g, x], send.at[2], asem.at[g], device)

    def mix(g):
        wait(r1.at[g, 0 : NX - 1], asem.at[g])
        u = [r1[g, s].astype(F32) for s in range(NX)]
        for s, w in enumerate(four(u)):
            wo[g, s] = (w * scale).astype(BF16)
        rot[g, x] = wo[g, x]
        for k in range(1, NX):
            xx, device = at_x(k)
            start(wo.at[g, xx], rot.at[g, x], send.at[3], bsem.at[g], device)

    for g in range(groups):
        transform(g)
    for s in (2, 3):
        sent.append((r1.at[:, 0 : NX - 1], s))

    wait(ybuf, recv.at[1])
    total = yp[some(y * yrows, yrows), :]
    for k in range(NY - 1):
        total = total + ybuf[k].astype(F32)
    zs[...] = total.astype(BF16)
    yp[0:yrows, :] = total
    for k in FAR_FIRST:
        zz, device = at_z(k)
        start(zs.at[some(zz * zrows, zrows), :], zbuf.at[k - 1], send.at[4], recv.at[4], device)
    sent.append((zbuf, 4))

    wait(zbuf, recv.at[4])
    total = yp[some(z * zrows, zrows), :]
    for k in range(NZ - 1):
        total = total + zbuf[k].astype(F32)
    own_rows = pl.multiple_of(y * yrows + z * zrows, zrows)
    own = yg.at[pl.ds(own_rows, zrows), :]
    own[...] = total.astype(BF16)
    for k in FAR_FIRST:
        start(own, own, send.at[5], recv.at[5], at_z(k)[1])
    sent.append((zbuf, 5))

    line = (2 * signs_ref[pl.ds(pos * 8 + own_rows // LANES, 1), :] - 1).astype(F32)
    spot = lax.broadcasted_iota(jnp.int32, (zrows, LANES), 0) + own_rows % LANES
    lane = lax.broadcasted_iota(jnp.int32, (zrows, LANES), 1)
    sign = jnp.sum(jnp.where(lane == spot, line, 0.0), axis=1, keepdims=True)
    vbuf[pos] = total * sign
    for k in range(1, NPOS):
        start(vbuf.at[pos], vbuf.at[pos], send.at[6], recv.at[6], at_pos(k))
    sent.append((vbuf.at[0 : NPOS - 1], 6))

    mix(0)
    wait(zbuf, recv.at[5])
    block = yg.at[some(y * yrows, yrows), :]
    for k in (2, 1, 3):
        start(block, block, send.at[7], recv.at[7], at_y(k)[1])
    sent.append((ybuf, 7))

    wait(vbuf.at[0 : NPOS - 1], recv.at[6])
    mixed = jnp.zeros((zrows, rank), F32)
    for s in range(NPOS):
        bits = (pos % 2) * (s % 2) + (pos // 2 % 2) * (s // 2 % 2) + (pos // 4) * (s // 4)
        mixed = mixed + vbuf[s] * (1 - 2 * (bits % 2)).astype(F32)
    own_v = vg.at[pl.ds(own_rows, zrows), :]
    own_v[...] = mixed.astype(BF16)
    for k in FAR_FIRST:
        start(own_v, own_v, send.at[8], recv.at[8], at_z(k)[1])
    sent.append((zbuf, 8))
    mix(1)

    wait(ybuf, recv.at[7])
    half, part = rank // NCORE, rank // NPOS
    ztp[...] = dot_t(yg[...], a_ref[...])
    start(ztp.at[some((1 - core) * half, half), :], ztc, send.at[10], recv.at[10], other_core)
    sent.append((ztc, 10))
    gs[...] = dot_t(yg[...], yg[...])
    start(gs, gcore, send.at[9], recv.at[9], other_core)
    sent.append((gs, 9))

    wait(ztc, recv.at[10])
    zh[...] = ztp[some(core * half, half), :] + ztc[...]
    for k in (2, 1, 3):
        xx, device = at_x(k)
        start(zh.at[some(xx * part, part), :], ztx.at[k - 1], send.at[13], recv.at[13], device)
    sent.append((ztx, 13))

    wait(gcore, recv.at[9])
    mine_half = some(core * half, half)
    gx[x] = gs[mine_half, :] + gcore[mine_half, :]
    for k in (2, 1, 3):
        start(gx.at[x], gx.at[x], send.at[12], recv.at[12], at_x(k)[1])
    sent.append((gx.at[0 : NX - 1], 12))
    mix(2)

    wait(ztx, recv.at[13])
    total = zh[some(x * part, part), :]
    for k in range(NX - 1):
        total = total + ztx[k]
    zx[...] = total
    start(zx, ztz, send.at[14], recv.at[14], other_rep)
    sent.append((zx, 14))

    wait(gx.at[0 : NX - 1], recv.at[12])
    gall[mine_half, :] = gx[0] + gx[1] + gx[2] + gx[3]
    own_g = gall.at[mine_half, :]
    start(own_g, own_g, send.at[11], recv.at[11], other_core)
    sent.append((own_g, 11))
    mix(3)

    wait(zbuf, recv.at[8])
    block_v = vg.at[some(y * yrows, yrows), :]
    for k in (2, 1, 3):
        start(block_v, block_v, send.at[17], recv.at[17], at_y(k)[1])
    sent.append((ybuf, 17))

    wait(own_g, recv.at[11])
    inverse_cholesky(gall[...], inv_ref, 4)
    inverse = inv_ref[...]
    mix(4)

    wait(ztz, recv.at[14])
    own_z = zta.at[pl.ds(pl.multiple_of(core * half + x * part, part), part), :]
    own_z[...] = zx[...] + ztz[...]
    for k in (2, 1, 3):
        start(own_z, own_z, send.at[15], recv.at[15], at_x(k)[1])
    sent.append((ztx, 15))
    mix(5)
    mix(6)

    wait(ybuf, recv.at[17])
    small16 = small.astype(BF16)
    t = [dot(small16, vg[a * SMALL : (a + 1) * SMALL, :]) for a in range(NX)]
    for a, v in enumerate(four(t)):
        basis_ref[a * SMALL : (a + 1) * SMALL, :] = lax.dot_general(
            v * scale, inverse, (((1,), (1,)), ((), ())), precision=HIGH, preferred_element_type=F32
        )

    wait(ztx, recv.at[15])
    half_z = zta.at[mine_half, :]
    start(half_z, half_z, send.at[16], recv.at[16], other_core)
    sent.append((ztc, 16))
    wait(ztc, recv.at[16])
    right = dot(inverse, zta[...], precision=HIGH) * (1.0 / REPLICAS)
    right16 = right.astype(BF16)
    for g in range(groups):
        qf_ref[lanes(g), :] = right[:, g * LANES : (g + 1) * LANES].T

    for g in range(groups):
        wait(rot.at[g, 0 : NX - 1], bsem.at[g])
        for a in range(NX):
            part_rows = pl.ds(a * SMALL, SMALL)
            approx = dot(basis_ref[part_rows, :].astype(BF16), right16[:, g * LANES : (g + 1) * LANES])
            err_ref[part_rows, lanes(g)] = (rot[g, a].astype(F32) - approx).astype(BF16)
    for ref, s in sent:
        wait(ref, send.at[s])


def local(accumulated, signs, q_start):
    rows, cols = accumulated.shape
    rank = q_start.shape[1]
    quarter, yrows = rows // NX, rows // NY
    zrows, half, part = yrows // NZ, rank // NCORE, rank // NPOS
    groups = cols // LANES
    vmem = pl.BlockSpec(memory_space=pltpu.VMEM)
    anywhere = pl.BlockSpec(memory_space=pl.ANY)
    dma = pltpu.SemaphoreType.DMA
    chunk = (groups, NX, quarter, LANES)
    scratch = [
        ((rows, cols), BF16), ((rows * NPOS // LANES, LANES), jnp.int32), ((cols, rank), BF16),
        ((groups, rows, LANES), BF16), (chunk, BF16), (chunk, BF16), (chunk, BF16), (chunk, BF16),
        ((2 * NX, SMALL, SMALL), BF16),
        ((rows, rank), F32), ((rows, rank), BF16), ((NY - 1, yrows, rank), BF16),
        ((yrows, rank), BF16), ((NZ - 1, zrows, rank), BF16), ((NPOS, zrows, rank), F32),
        ((rows, rank), BF16), ((rows, rank), BF16),
        ((rank, rank), F32), ((rank, rank), F32), ((NX, half, rank), F32), ((rank, rank), F32),
        ((rank, cols), F32), ((half, cols), F32), ((half, cols), F32), ((NX - 1, part, cols), F32),
        ((part, cols), F32), ((part, cols), F32), ((rank, cols), F32), ((rank, rank), F32),
    ]
    return pl.pallas_call(
        kernel,
        out_shape=(
            jax.ShapeDtypeStruct((rows, cols), BF16),
            jax.ShapeDtypeStruct((rows, rank), F32),
            jax.ShapeDtypeStruct((cols, rank), F32),
        ),
        in_specs=[anywhere] * 3,
        out_specs=(vmem,) * 3,
        scratch_shapes=[pltpu.VMEM(shape, kind) for shape, kind in scratch]
        + [dma((18,)), dma((18,)), dma((groups,)), dma((groups,)), dma((groups,)), dma((3,))],
        compiler_params=pltpu.CompilerParams(
            collective_id=0, has_side_effects=True, vmem_limit_bytes=48 * 1024 * 1024
        ),
        name="powersgd",
    )(accumulated, signs.reshape(-1, LANES), q_start)


def solution(mesh):
    in_specs = (P("dp", "mp"), P(), P("mp", None))
    out_specs = (P("dp", "mp"), P("dp", None), P("mp", None))
    return jax.shard_map(local, mesh=mesh, in_specs=in_specs, out_specs=out_specs, check_vma=False)
```

time: 87.2 us -> 79.3 us (0.909)
  Pallas kernels: 80.3 us -> 72.4 us
    pallas_call x1, Pallas kernels: 80.3 us -> 72.4 us  [local(): pl.pallas_call(kernel, out_shape=(jax.ShapeDtypeStruct((rows, cols), BF16...]
where the time goes in v2:
time: 79.3 us; the launch traced here: 79.1 us
  Pallas kernels  72.4 us (91%)
  local copies, waits for them, and re-layouts  5.98 us (8%)
    pallas_call x1, Pallas kernels, local(): pl.pallas_call(kernel, out_shape=(jax.ShapeDtypeStruct((rows, cols), BF16...  72.4 us
    unnamed x9, local copies, waits for them, and re-layouts  5.98 us

profile of v2, /device:TPU:1, one launch (start us, length us, event | category | flops | bytes accessed | tf_op | source)
XLA Modules:
  0.0 79.1 jit_solution(4833831446290255846)
XLA Ops:
  0.6 0.0 copy-start
  0.6 1.5 %copy-done = bf16[1024,896]{1,0:T(8,128)(2,1)S(1)} copy-done((bf16[1024,896]{1,0:T(8,128)(2,1)S(1)}, bf16[1024,896]{1,0:T(8,128)(2,1)}, u32[]{:S(2)}) %copy-start) | copy-done | bytes 1835032
  2.1 0.0 copy-start.1
  2.1 0.9 %copy-done.1 = bf16[896,128]{1,0:T(8,128)(2,1)S(1)} copy-done((bf16[896,128]{1,0:T(8,128)(2,1)S(1)}, bf16[896,128]{1,0:T(8,128)(2,1)}, u32[]{:S(2)}) %copy-start.1) | copy-done | bytes 229400
  3.1 0.0 copy-start.2
  3.1 0.8 copy-done.2
  3.8 72.4 %powersgd.1 = (bf16[1024,896]{1,0:T(8,128)(2,1)S(1)}, f32[1024,128]{1,0:T(8,128)S(1)}, f32[896,128]{1,0:T(8,128)S(1)}) custom-call(bf16[1024,896]{1,0:T(8,128)(2,1)S(1)} %copy-done, s32[64,128]{1,0:T(8,128)S(1)} %bitcast.1, bf16[896,128]{1,0:T(8,128)(2,1)S(1)} %copy-done.1), custom_call_target="tpu_custom_call" | custom-call | tf_op jit(solution)/shard_map/powersgd/pallas_call | solution.py:356
  76.3 1.2 %copy.9 = bf16[1024,896]{1,0:T(8,128)(2,1)} copy(bf16[1024,896]{1,0:T(8,128)(2,1)S(1)} %get-tuple-element.6) | data formatting | bytes 3670016
  77.5 0.8 %copy.10 = f32[1024,128]{1,0:T(8,128)} copy(f32[1024,128]{1,0:T(8,128)S(1)} %get-tuple-element.7) | data formatting | bytes 1048576
  78.3 0.8 copy.11
Async XLA Ops:
  0.6 1.5 %copy-start = (bf16[1024,896]{1,0:T(8,128)(2,1)S(1)}, bf16[1024,896]{1,0:T(8,128)(2,1)}, u32[]{:S(2)}) copy-start(bf16[1024,896]{1,0:T(8,128)(2,1)} %a_hbm.1) | copy-start | bytes 5505028
  2.1 0.9 %copy-start.1 = (bf16[896,128]{1,0:T(8,128)(2,1)S(1)}, bf16[896,128]{1,0:T(8,128)(2,1)}, u32[]{:S(2)}) copy-start(bf16[896,128]{1,0:T(8,128)(2,1)} %q_hbm.1) | copy-start | bytes 688132
  3.1 0.8 copy-start.2
